TPU v7x, 512 devices: a whole 4x4x16 slice. The times are simulated.
512 devices in a mesh: dp: 64 (over z_hi, y, x, core), mp: 8 (over z_lo).
Axes of the slice: x: 4, y: 4, z: 16 (z_hi: 2, z_lo: 8; z = z_hi * 8 + z_lo), core: 2. Of those that a mesh axis runs over, the one named last changes fastest.
Arguments:
- image_feats: bfloat16 [8192, 1792], P('dp'), may hold values from -6 to 6
- text_feats: bfloat16 [8192, 2048], P('dp'), may hold values from -6 to 6
- image_proj: bfloat16 [1792, 1152], P('mp'), may hold values from -0.125 to 0.125
- text_proj: bfloat16 [2048, 1152], P('mp'), may hold values from -0.125 to 0.125
- log_scale: float32 [1], replicated, may hold values from 2 to 2.8
- logit_bias: float32 [1], replicated, may hold values from -7 to -4
Outputs:
- grad_image: float32 [1792, 1152], P('mp')
- grad_text: float32 [2048, 1152], P('mp')
All inputs are finite; a program needn't handle non-finite values.
Results may differ from a plain program's by a relative error of at most 0.004.
Values may be sent and summed in bfloat16 or wider, within the bound.
A program may use at most 64 MiB of HBM per device.

v0:
```python
import jax
import jax.numpy as jnp
from jax import lax
from jax.sharding import PartitionSpec as P

norm_eps = 1e-06


def pair_weights(left_rows, right_rows, left_ids, right_ids, scale_value, bias_value):
    logits = (
        scale_value
        * lax.dot_general(
            left_rows, right_rows, (((1,), (1,)), ((), ())), preferred_element_type=jnp.float32
        )
        + bias_value
    )
    matched = left_ids[:, None] == right_ids[None, :]
    slopes = jnp.where(matched, -jax.nn.sigmoid(-logits), jax.nn.sigmoid(logits))
    return (scale_value * slopes).astype(jnp.bfloat16)


def visiting_ids(count, share_rows, row_count, model_rank):
    position = jnp.arange(count, dtype=jnp.int32)
    return position // share_rows * row_count + model_rank * share_rows + position % share_rows


def on_device(image_feats, text_feats, image_proj, text_proj, log_scale, logit_bias):
    model_rank = lax.axis_index("mp")
    data_rank = lax.axis_index("dp")
    model_parts = lax.axis_size("mp")
    row_count = image_feats.shape[0]
    share_rows = row_count // model_parts
    embed_width = image_proj.shape[1]
    image_width = image_proj.shape[0]
    text_width = text_proj.shape[0]
    image_cols = lax.dynamic_slice_in_dim(image_feats, model_rank * image_width, image_width, 1)
    text_cols = lax.dynamic_slice_in_dim(text_feats, model_rank * text_width, text_width, 1)
    projected = lax.psum_scatter(
        jnp.concatenate(
            [
                jnp.dot(image_cols, image_proj, preferred_element_type=jnp.float32),
                jnp.dot(text_cols, text_proj, preferred_element_type=jnp.float32),
            ],
            1,
        ),
        "mp",
        scatter_dimension=0,
        tiled=True,
    )
    pre_image = projected[:, :embed_width]
    pre_text = projected[:, embed_width:]
    inv_image = lax.rsqrt(jnp.sum(pre_image * pre_image, 1) + norm_eps)
    inv_text = lax.rsqrt(jnp.sum(pre_text * pre_text, 1) + norm_eps)
    unit_image = pre_image * inv_image[:, None]
    unit_text = pre_text * inv_text[:, None]
    own_image = unit_image.astype(jnp.bfloat16)
    own_text = unit_text.astype(jnp.bfloat16)
    full_image, full_text = (
        lax.all_gather(own_image, "mp", axis=0, tiled=True),
        lax.all_gather(own_text, "mp", axis=0, tiled=True),
    )
    scale_value = jnp.exp(log_scale[0])
    bias_value = logit_bias[0]
    home_ids = data_rank * row_count + jnp.arange(row_count, dtype=jnp.int32)
    visiting = lax.all_gather(own_text, "dp", axis=0, tiled=True)
    text_ids = visiting_ids(visiting.shape[0], share_rows, row_count, model_rank)
    weights = pair_weights(full_image, visiting, home_ids, text_ids, scale_value, bias_value)
    dz_image = jnp.dot(weights, visiting, preferred_element_type=jnp.float32)
    visiting = lax.all_gather(own_image, "dp", axis=0, tiled=True)
    image_ids = visiting_ids(visiting.shape[0], share_rows, row_count, model_rank)
    weights = pair_weights(visiting, full_text, image_ids, home_ids, scale_value, bias_value)
    dz_text = lax.dot_general(
        weights, visiting, (((0,), (0,)), ((), ())), preferred_element_type=jnp.float32
    )
    image_grads, text_grads = (
        lax.psum_scatter(dz_image, "mp", scatter_dimension=0, tiled=True),
        lax.psum_scatter(dz_text, "mp", scatter_dimension=0, tiled=True),
    )
    image_dots = jnp.sum(image_grads * unit_image, 1)
    text_dots = jnp.sum(text_grads * unit_text, 1)
    back_image = (inv_image[:, None] * (image_grads - unit_image * image_dots[:, None])).astype(
        jnp.bfloat16
    )
    back_text = (inv_text[:, None] * (text_grads - unit_text * text_dots[:, None])).astype(
        jnp.bfloat16
    )
    whole_image, whole_text = (
        lax.all_gather(back_image, "mp", axis=0, tiled=True),
        lax.all_gather(back_text, "mp", axis=0, tiled=True),
    )
    local_image = jnp.dot(image_cols.T, whole_image, preferred_element_type=jnp.float32)
    local_text = jnp.dot(text_cols.T, whole_text, preferred_element_type=jnp.float32)
    grad_image, grad_text = lax.psum((local_image, local_text), "dp")
    return (grad_image, grad_text)


def solution(mesh):
    placed = (P("dp", None), P("dp", None), P("mp", None), P("mp", None), P(), P())
    return jax.shard_map(
        on_device,
        mesh=mesh,
        in_specs=placed,
        out_specs=(P("mp", None), P("mp", None)),
        check_vma=False,
    )
```

profile of v0, /device:TPU:1, one launch (start us, length us, event | category | flops | bytes accessed | tf_op | source)
XLA Modules:
  0.0 1601.1 jit_solution(6514008878978170726)
XLA Ops:
  7.2 1.4 fusion.22
  8.7 1.1 fusion.18
  9.8 1.1 pad_maximum_fusion
  10.9 68.2 %reduce-scatter.4.cloned.1.call-done = f32[16,2304]{1,0:T(8,128)} async-done(((f32[128,2304]{1,0:T(8,128)}), f32[16,2304]{1,0:T(8,128)}) %reduce-scatter.4.cloned.1.call-update) | async-done | bytes 147472 | tf_op jit(solution)/shard_map/reduce_scatter | solution.py:38
  79.2 1.0 multiply_reduce_fusion.3
  80.2 1.6 fusion.24
  81.9 0.7 all-gather.5.cloned.1.call-update
  84.0 41.7 %all_gather.18 = bf16[128,1152]{1,0:T(8,128)(2,1)S(1)} all-gather(bf16[16,1152]{1,0:T(8,128)(2,1)} %get-tuple-element.10), channel_id=1, replica_groups=mesh['dp'=64,'mp'=8] {'mp'}, dimensions={0}, use_global_device_ids=true | all-gather | bytes 331776 | tf_op jit(solution)/shard_map/all_gather | solution.py:59
  125.7 72.4 %all-gather.3.cloned.1.call-done = bf16[1024,1152]{1,0:T(8,128)(2,1)} async-done(((bf16[16,1152]{1,0:T(8,128)(2,1)}), bf16[1024,1152]{1,0:T(8,128)(2,1)}) %all-gather.3.cloned.1.call-update) | async-done | bytes 2359312 | tf_op jit(solution)/shard_map/all_gather | solution.py:65
  198.2 4.6 fusion.3
  202.9 40.9 %all_gather.22 = bf16[128,1152]{1,0:T(8,128)(2,1)S(1)} all-gather(bf16[16,1152]{1,0:T(8,128)(2,1)S(1)} %copy-done.3), channel_id=1, replica_groups=mesh['dp'=64,'mp'=8] {'mp'}, dimensions={0}, use_global_device_ids=true | all-gather | bytes 331776 | tf_op jit(solution)/shard_map/all_gather | solution.py:60
  243.8 63.2 %all-gather.5.cloned.1.call-done = bf16[1024,1152]{1,0:T(8,128)(2,1)} async-done(((bf16[16,1152]{1,0:T(8,128)(2,1)}), bf16[1024,1152]{1,0:T(8,128)(2,1)}) %all-gather.5.cloned.1.call-update) | async-done | bytes 2359312 | tf_op jit(solution)/shard_map/all_gather | solution.py:69
  307.0 5.0 fusion.2
  312.1 46.3 %reduce-scatter.6.cloned.1.call-done = f32[16,1152]{1,0:T(8,128)} async-done(((f32[128,1152]{1,0:T(8,128)}), f32[16,1152]{1,0:T(8,128)}) %reduce-scatter.6.cloned.1.call-update) | async-done | bytes 73744 | tf_op jit(solution)/shard_map/reduce_scatter | solution.py:76
  358.4 62.0 %reduce-scatter.8.cloned.1.call-done = f32[16,1152]{1,0:T(8,128)} async-done(((f32[128,1152]{1,0:T(8,128)}), f32[16,1152]{1,0:T(8,128)}) %reduce-scatter.8.cloned.1.call-update) | async-done | bytes 73744 | tf_op jit(solution)/shard_map/reduce_scatter | solution.py:77
  420.4 1.1 multiply_reduce_fusion
  421.5 1.0 multiply_convert_fusion.2
  422.6 40.9 %all_gather.23 = bf16[128,1152]{1,0:T(8,128)(2,1)S(1)} all-gather(bf16[16,1152]{1,0:T(8,128)(2,1)S(1)} %get-tuple-element.8), channel_id=1, replica_groups=mesh['dp'=64,'mp'=8] {'mp'}, dimensions={0}, use_global_device_ids=true | all-gather | bytes 331776 | tf_op jit(solution)/shard_map/all_gather | solution.py:89
  463.4 2.2 fusion.16
  465.6 40.6 %all_gather.20 = bf16[128,1152]{1,0:T(8,128)(2,1)S(1)} all-gather(bf16[16,1152]{1,0:T(8,128)(2,1)S(1)} %get-tuple-element.9), channel_id=1, replica_groups=mesh['dp'=64,'mp'=8] {'mp'}, dimensions={0}, use_global_device_ids=true | all-gather | bytes 331776 | tf_op jit(solution)/shard_map/all_gather | solution.py:88
  506.2 2.2 fusion.20
  508.5 1082.4 %all-reduce.3.cloned.1.call-done = (f32[224,1152]{1,0:T(8,128)}, f32[256,1152]{1,0:T(8,128)}) async-done(((f32[224,1152]{1,0:T(8,128)}, f32[256,1152]{1,0:T(8,128)}), (f32[224,1152]{1,0:T(8,128)}, f32[256,1152]{1,0:T(8,128)})) %all-reduce.3.cloned.1.call-update) | async-done | bytes 2211856 | tf_op jit(solution)/shard_map/psum | solution.py:93
  1590.9 2.3 copy.12
  1593.3 1.0 copy.13
  (22 shorter events, 0.4 us)
Async XLA Ops:
  7.2 1.5 copy-start
  7.2 72.0 %reduce-scatter.4.cloned.1.call-start = ((), (), s32[]{:S(2)}) async-start(), calls=%async_computation.3 | async-start | bytes 1327104 | tf_op jit(solution)/shard_map/reduce_scatter | solution.py:38
  10.9 187.3 %all-gather.3.cloned.1.call-start = ((), (), s32[]{:S(2)}) async-start(), calls=%async_computation.4 | async-start | bytes 2396160 | tf_op jit(solution)/shard_map/all_gather | solution.py:65
  81.9 225.2 %all-gather.5.cloned.1.call-start = ((), (), s32[]{:S(2)}) async-start(), calls=%async_computation.6 | async-start | bytes 2396160 | tf_op jit(solution)/shard_map/all_gather | solution.py:69
  82.6 275.8 %reduce-scatter.6.cloned.1.call-start = ((), (), s32[]{:S(2)}) async-start(), calls=%async_computation.5 | async-start | bytes 663552 | tf_op jit(solution)/shard_map/reduce_scatter | solution.py:76
  198.2 4.7 copy-start.3
  202.8 217.6 %reduce-scatter.8.cloned.1.call-start = ((), (), s32[]{:S(2)}) async-start(), calls=%async_computation.7 | async-start | bytes 663552 | tf_op jit(solution)/shard_map/reduce_scatter | solution.py:77
  307.0 113.4 %copy-start.1 = (f32[16,2304]{1,0:T(8,128)S(1)}, f32[16,2304]{1,0:T(8,128)}, u32[]{:S(2)}) copy-start(f32[16,2304]{1,0:T(8,128)} %reduce-scatter.4.cloned.1.call-done) | copy-start | bytes 442372
  312.0 1278.9 %all-reduce.3.cloned.1.call-start = ((), (), s32[]{:S(2)}) async-start(), calls=%async_computation.8 | async-start | bytes 4423680 | tf_op jit(solution)/shard_map/psum | solution.py:93
  1590.9 2.3 copy-start.2
Sparse Core Ops, SparseCore 0:
  11.4 67.7 reduce-scatter.3
  83.6 114.4 all-gather.2
  203.2 103.7 all-gather.4
  310.3 48.0 reduce-scatter.5
  361.7 58.7 reduce-scatter.7
  508.6 1082.2 all-reduce.2
where the time goes:
time: 1600 us
  waiting for transfers between devices  1400 us (88%)
  blocking collectives  164 us (10%)
  matrix products  16.6 us (1%)
    psum x1, waiting for transfers between devices, on_device(): grad_image, grad_text = lax.psum((local_image, local_text), 'dp')  1080 us
    all_gather x1, waiting for transfers between devices, on_device(): visiting = lax.all_gather(own_text, 'dp', axis=0, tiled=True)  72.4 us
    reduce_scatter x1, waiting for transfers between devices, on_device(): lax.psum_scatter(jnp.concatenate([jnp.dot(image_cols, image_proj, preferr...  68.2 us
    all_gather x1, waiting for transfers between devices, on_device(): visiting = lax.all_gather(own_image, 'dp', axis=0, tiled=True)  63.2 us
    reduce_scatter x1, waiting for transfers between devices, on_device(): lax.psum_scatter(dz_text, 'mp', scatter_dimension=0, tiled=True)  62 us
    reduce_scatter x1, waiting for transfers between devices, on_device(): lax.psum_scatter(dz_image, 'mp', scatter_dimension=0, tiled=True)  46.3 us
    all_gather x1, blocking collectives, on_device(): lax.all_gather(own_image, 'mp', axis=0, tiled=True)  41.7 us
    all_gather x1, blocking collectives, on_device(): lax.all_gather(own_text, 'mp', axis=0, tiled=True)  40.9 us
  transfers between devices with their start and end apart: 6, of which 6 were waited for; matrix products, arithmetic and copies ran while one was open for 1% of the time, Pallas kernels for 0%

commit v1 on v0

v1 whole, which is shorter than its diff:
```python
import jax
import jax.numpy as jnp
from jax import lax
from jax.experimental import pallas as pl
from jax.experimental.pallas import tpu as pltpu
from jax.sharding import PartitionSpec as P

norm_eps = 1e-06
f32, bf16 = jnp.float32, jnp.bfloat16
MESH = pl.DeviceIdType.MESH
E = 1152
plane_offsets = [(dx, dy) for dx in range(4) for dy in range(4)]
plane_order = sorted(range(1, 16), key=lambda p: -sum(min(o, 4 - o) for o in plane_offsets[p]))
line_order = [4, 3, 5, 2, 6, 1, 7]


def device_at(x, y, z, c):
    z_hi, z_lo = z // 8, lax.rem(z, 8)
    return {"dp": ((z_hi * 4 + y) * 4 + x) * 2 + c, "mp": z_lo}


def dot(a, b, dims):
    return lax.dot_general(a, b, (dims, ((), ())), preferred_element_type=f32)


def kernel(
    fi, ft, wi, wt, ls, lb, out,
    part, part_in, images, texts, dz_i, dz_t, dz_i_wire, dz_i_in, swap_out, swap_in,
    text_sib_in, dz_t_wire, dz_t_in, back_i, back_t, grads, grads_sib_in, grads_wire,
    grads_in, zsum_out, zsum_in, result,
    s1, r1, st, rt, sx, rx, ss, rs, si, ri, sdi, rdi, sdt, rdt, sb, rb, sg, rg, so, ro, sm, rm,
):
    d, z_lo = lax.axis_index("dp"), lax.axis_index("mp")
    c, x, y, z_hi = lax.rem(d, 2), lax.rem(d // 2, 4), lax.rem(d // 8, 4), d // 32
    z = z_hi * 8 + z_lo
    sibling = device_at(x, y, z, 1 - c)
    pair = device_at(x, y, z + 1 - 2 * lax.rem(z, 2), c)
    far = device_at(x, y, lax.rem(z + 8, 16), c)

    def line(j):
        return device_at(x, y, z_hi * 8 + lax.rem(z_lo + j, 8), c)

    def stride(k):
        return device_at(x, y, lax.rem(z + 2 * k, 16), c)

    def plane(p):
        dx, dy = plane_offsets[p]
        return device_at(lax.rem(x + dx, 4), lax.rem(y + dy, 4), z, c)

    def plane_back(p):
        dx, dy = plane_offsets[p]
        return device_at(lax.rem(x + 4 - dx, 4), lax.rem(y + 4 - dy, 4), z, c)

    def plane_index(p):
        dx, dy = plane_offsets[p]
        return lax.rem(x + dx, 4) * 4 + lax.rem(y + dy, 4)

    def send(src, dst, s, r, to):
        cp = pltpu.make_async_remote_copy(
            src_ref=src, dst_ref=dst, send_sem=s, recv_sem=r, device_id=to, device_id_type=MESH
        )
        cp.start()
        return cp

    partners = [line(j) for j in range(1, 8)]
    partners += [device_at(x, y, (1 - z_hi) * 8 + lax.rem(z_lo + 2 * j, 8), c) for j in range(4)]
    partners += [plane(p) for p in range(1, 16)] + [sibling]
    barrier = pltpu.get_barrier_semaphore()
    for to in partners:
        pl.semaphore_signal(barrier, inc=1, device_id=to, device_id_type=MESH)

    part[:, :E] = dot(fi[:, :224], wi[...], ((1,), (0,))).astype(part.dtype)
    part[:, E:] = dot(ft[...], wt[...], ((1,), (0,))).astype(part.dtype)
    pl.semaphore_wait(barrier, len(partners))

    sends = []
    for j in line_order:
        rows = pl.ds(pl.multiple_of(lax.rem(z_lo + j, 8) * 16, 16), 16)
        sends.append(send(part.at[rows], part_in.at[j - 1], s1.at[j - 1], r1.at[j - 1], line(j)))
    pre = part[pl.ds(pl.multiple_of(z_lo * 16, 16), 16), :].astype(f32)
    for cp in sends:
        cp.wait()
    for j in range(7):
        pre = pre + part_in[j].astype(f32)

    pre_i, pre_t = pre[:, :E], pre[:, E:]
    inv_i = lax.rsqrt(jnp.sum(pre_i * pre_i, 1, keepdims=True) + norm_eps)
    inv_t = lax.rsqrt(jnp.sum(pre_t * pre_t, 1, keepdims=True) + norm_eps)
    unit_i, unit_t = pre_i * inv_i, pre_t * inv_t
    images[0:16, :] = unit_i.astype(bf16)
    texts[0:16, :] = unit_t.astype(bf16)

    swap = send(images.at[pl.ds(0, 16)], images.at[pl.ds(16, 16)], sx.at[0], rx.at[0], pair)
    tsends = {}
    for k in line_order:
        tsends[k] = send(texts.at[pl.ds(0, 16)], texts.at[pl.ds(16 * k, 16)], st.at[k], rt.at[k], stride(k))
    sib = [send(texts.at[pl.ds(0, 16)], texts.at[pl.ds(128, 16)], ss.at[0], rs.at[0], sibling)]
    isends = []
    for p in plane_order:
        isends.append(send(images.at[pl.ds(0, 16)], images.at[pl.ds(32 * p, 16)], si.at[0, p], ri.at[0, p], plane(p)))
    swap.wait()
    for p in plane_order:
        isends.append(send(images.at[pl.ds(16, 16)], images.at[pl.ds(32 * p + 16, 16)], si.at[1, p], ri.at[1, p], plane(p)))
    for k in (1, 7, 2, 6, 3, 5, 4):
        tsends[k].wait()
        sib.append(send(texts.at[pl.ds(16 * k, 16)], texts.at[pl.ds(128 + 16 * k, 16)], ss.at[k], rs.at[k], sibling))
    for cp in sib + isends:
        cp.wait()

    scale = jnp.exp(jnp.full((8, 128), ls[0], f32))[0:1, 0:1]
    bias = lb[0]
    dz_t[...] = jnp.zeros_like(dz_t)

    def chunk(i, carry):
        rows = pl.ds(pl.multiple_of(i * 128, 128), 128)
        mine, every = images[rows, :], texts[...]
        logits = scale * dot(mine, every, ((1,), (1,))) + bias
        row = lax.broadcasted_iota(jnp.int32, (128, 256), 0) + i * 128
        col = lax.broadcasted_iota(jnp.int32, (128, 256), 1)
        matched = (row == col) & (row < 16)
        sig = jax.nn.sigmoid(jnp.where(matched, -logits, logits))
        weights = (scale * jnp.where(matched, -sig, sig)).astype(bf16)
        dz_i[rows, :] = dot(weights, every, ((1,), (0,)))
        dz_t[...] += dot(weights, mine, ((0,), (0,)))
        return carry

    lax.fori_loop(0, 4, chunk, 0)

    tsib = send(dz_t.at[pl.ds(128, 128)], text_sib_in, ss.at[8], rs.at[8], sibling)
    dz_i_wire[...] = dz_i[...].astype(dz_i_wire.dtype)
    dsends = []
    for p in plane_order:
        dsends.append(send(dz_i_wire.at[pl.ds(32 * p, 32)], dz_i_in.at[p], sdi.at[p], rdi.at[p], plane_back(p)))
    tsib.wait()
    dz_text = dz_t[0:128, :] + text_sib_in[...]
    dz_t_wire[...] = dz_text.astype(dz_t_wire.dtype)
    dtsends = []
    for k in line_order:
        dtsends.append(send(dz_t_wire.at[pl.ds(16 * k, 16)], dz_t_in.at[k], sdt.at[k], rdt.at[k], stride(8 - k)))
    sum_i = dz_i[0:32, :]
    for cp in dsends:
        cp.wait()
    for p in range(1, 16):
        sum_i = sum_i + dz_i_in[p].astype(f32)
    swap_out[...] = sum_i[16:32, :]
    swap = send(swap_out, swap_in, sx.at[1], rx.at[1], pair)
    sum_t = dz_text[0:16, :]
    for cp in dtsends:
        cp.wait()
    for k in range(1, 8):
        sum_t = sum_t + dz_t_in[k].astype(f32)
    swap.wait()
    sum_i = sum_i[0:16, :] + swap_in[...]

    dots_i = jnp.sum(sum_i * unit_i, 1, keepdims=True)
    dots_t = jnp.sum(sum_t * unit_t, 1, keepdims=True)
    own = pl.ds(pl.multiple_of(z_lo * 16, 16), 16)
    back_i[own, :] = (inv_i * (sum_i - unit_i * dots_i)).astype(bf16)
    back_t[own, :] = (inv_t * (sum_t - unit_t * dots_t)).astype(bf16)
    bsends = []
    for j in line_order:
        bsends.append(send(back_i.at[own], back_i.at[own], sb.at[0, j - 1], rb.at[0, j - 1], line(j)))
        bsends.append(send(back_t.at[own], back_t.at[own], sb.at[1, j - 1], rb.at[1, j - 1], line(j)))
    for cp in bsends:
        cp.wait()

    grads[0:8] = dot(fi[...], back_i[...], ((0,), (0,))).reshape(8, 32, E)
    grads[8:16] = dot(ft[...], back_t[...], ((0,), (0,))).reshape(8, 32, E)
    give = pl.ds(pl.multiple_of((1 - c) * 16, 16), 16)
    keep = pl.ds(pl.multiple_of(c * 16, 16), 16)
    gsib = send(grads.at[:, give], grads_sib_in, sm.at[0], rm.at[0], sibling)
    gsib.wait()
    me = plane_index(0)

    def add_tile(t, carry):
        grads_wire[t] = (grads[t, keep, :] + grads_sib_in[t]).astype(grads_wire.dtype)
        return carry

    lax.fori_loop(0, 16, add_tile, 0)
    gsends = []
    for p in plane_order:
        gsends.append(send(grads_wire.at[plane_index(p)], grads_in.at[p], sg.at[p], rg.at[p], plane(p)))
    total = grads[me, keep, :] + grads_sib_in[me]
    for cp in gsends:
        cp.wait()
    for p in range(1, 16):
        total = total + grads_in[p].astype(f32)
    zsum_out[...] = total
    zs = send(zsum_out, zsum_in, sm.at[1], rm.at[1], far)
    zs.wait()
    result[me, c] = (total + zsum_in[...]).astype(result.dtype)
    tile = result.at[me, c]
    osends = []
    for p in plane_order:
        osends.append(send(tile, tile, so.at[p], ro.at[p], plane(p)))
    for cp in osends:
        cp.wait()
    whole = send(result.at[:, c], result.at[:, c], sm.at[2], rm.at[2], sibling)
    whole.wait()
    out[...] = result[...].reshape(512, E)


def on_device(image_feats, text_feats, image_proj, text_proj, log_scale, logit_bias):
    m = lax.axis_index("mp")
    fi = jnp.pad(lax.dynamic_slice_in_dim(image_feats, m * 224, 224, 1), ((0, 0), (0, 32)))
    ft = lax.dynamic_slice_in_dim(text_feats, m * 256, 256, 1)
    dma = pltpu.SemaphoreType.DMA
    vmem = pltpu.VMEM
    wire_1, wire_dz, wire_g, wire_o = f32, bf16, bf16, bf16
    grads = pl.pallas_call(
        kernel,
        out_shape=jax.ShapeDtypeStruct((512, E), wire_o),
        in_specs=[pl.BlockSpec(memory_space=vmem)] * 4 + [pl.BlockSpec(memory_space=pltpu.SMEM)] * 2,
        out_specs=pl.BlockSpec(memory_space=vmem),
        scratch_shapes=[
            vmem((128, 2 * E), wire_1), vmem((7, 16, 2 * E), wire_1),
            vmem((512, E), bf16), vmem((256, E), bf16),
            vmem((512, E), f32), vmem((256, E), f32),
            vmem((512, E), wire_dz), vmem((16, 32, E), wire_dz),
            vmem((16, E), f32), vmem((16, E), f32),
            vmem((128, E), f32), vmem((128, E), wire_dz), vmem((8, 16, E), wire_dz),
            vmem((128, E), bf16), vmem((128, E), bf16),
            vmem((16, 32, E), f32), vmem((16, 16, E), f32), vmem((16, 16, E), wire_g),
            vmem((16, 16, E), wire_g), vmem((16, E), f32), vmem((16, E), f32),
            vmem((16, 2, 16, E), wire_o),
            dma((7,)), dma((7,)), dma((8,)), dma((8,)), dma((2,)), dma((2,)), dma((9,)), dma((9,)),
            dma((2, 16)), dma((2, 16)), dma((16,)), dma((16,)), dma((8,)), dma((8,)),
            dma((2, 7)), dma((2, 7)), dma((16,)), dma((16,)), dma((16,)), dma((16,)), dma((3,)), dma((3,)),
        ],
        compiler_params=pltpu.CompilerParams(
            collective_id=0, has_side_effects=True, vmem_limit_bytes=48 * 2**20
        ),
        name="heads",
    )(fi, ft, image_proj, text_proj, log_scale, logit_bias)
    return grads[:224].astype(f32), grads[256:].astype(f32)


def solution(mesh):
    placed = (P("dp", None), P("dp", None), P("mp", None), P("mp", None), P(), P())
    return jax.shard_map(
        on_device,
        mesh=mesh,
        in_specs=placed,
        out_specs=(P("mp", None), P("mp", None)),
        check_vma=False,
    )
```

time: 1600 us -> 180 us (0.11)
  the two profiles are of different devices: /device:TPU:1 before, /device:TPU:97 now
where the time goes in v1:
time: 180 us
  Pallas kernels  173 us (96%)
  local copies, waits for them, and re-layouts  3.13 us (2%)
  other arithmetic  2.12 us (1%)
  between operations  2.04 us (1%)
    pallas_call x1, Pallas kernels, on_device(): pl.pallas_call(kernel, out_shape=jax.ShapeDtypeStruct((512, E), wire_o),...  173 us

profile of v1, /device:TPU:97, one launch (start us, length us, event | category | flops | bytes accessed | tf_op | source)
XLA Modules:
  0.0 180.1 jit_solution(17425570111707190857)
XLA Ops:
  0.6 0.0 copy-start
  2.0 1.0 constant_dynamic-slice_fusion.1
  3.0 0.0 copy-done
  3.0 0.0 copy-start.1
  3.1 1.1 copy-done.1
  4.1 0.0 copy-start.2
  4.1 1.0 copy-done.2
  5.2 172.8 %heads.1 = bf16[512,1152]{1,0:T(8,128)(2,1)S(1)} custom-call(bf16[128,256]{1,0:T(8,128)(2,1)S(1)} %pad.4.fi, bf16[128,256]{1,0:T(8,128)(2,1)S(1)} %constant_dynamic-slice_fusion.ft, bf16[224,1152]{1,0:T(8,128)(2,1)S(1)} %copy-done.2, bf16[256,1152]{1,0:T(8,128)(2,1)S(1)} %copy-done.1, f32[1]{0:T(128)S(6)} %copy.8.ls, f32[1]{0:T(128)S(6)} %copy.9.lb), custom_call_target="tpu_custom_call" | custom-call | tf_op jit(solution)/shard_map/heads/pallas_call | solution.py:210
  178.0 1.0 slice_convert_fusion.1
  179.0 1.1 slice_convert_fusion
  (2 shorter events, 0.0 us)
Async XLA Ops:
  0.6 2.4 %copy-start = (bf16[128,2048]{1,0:T(8,128)(2,1)S(1)}, bf16[128,2048]{1,0:T(8,128)(2,1)}, u32[]{:S(2)}) copy-start(bf16[128,2048]{1,0:T(8,128)(2,1)} %param.7) | copy-start | bytes 1572868
  3.0 1.1 copy-start.1
  4.1 1.0 copy-start.2

commit v2 on v1

--- a/solution.py
+++ b/solution.py
@@ -24,21 +24,22 @@
 
 
 def kernel(
-    fi, ft, wi, wt, ls, lb, out,
-    part, part_in, images, texts, dz_i, dz_t, dz_i_wire, dz_i_in, swap_out, swap_in,
-    text_sib_in, dz_t_wire, dz_t_in, back_i, back_t, grads, grads_sib_in, grads_wire,
+    fi_hbm, ft_hbm, wi_hbm, wt_hbm, ls, lb, out,
+    fi, ft, wi, wt, part, acc_1, acc_2, in_1, in_2, in_3,
+    images, texts, dz_i, dz_t, dz_i_wire, dz_i_in, swap_out, swap_in,
+    text_sib_in, dz_t_wire, dz_t_in, back, grad_i, grads, grads_sib_in, grads_wire,
     grads_in, zsum_out, zsum_in, result,
-    s1, r1, st, rt, sx, rx, ss, rs, si, ri, sdi, rdi, sdt, rdt, sb, rb, sg, rg, so, ro, sm, rm,
+    sl, s1, r1, st, rt, sx, rx, ss, rs, si, ri, sdi, rdi, sdt, rdt, sb, rb, sg, rg, so, ro, sm, rm,
 ):
     d, z_lo = lax.axis_index("dp"), lax.axis_index("mp")
     c, x, y, z_hi = lax.rem(d, 2), lax.rem(d // 2, 4), lax.rem(d // 8, 4), d // 32
     z = z_hi * 8 + z_lo
+    b0, b1, b2 = lax.rem(z_lo, 2), lax.rem(z_lo // 2, 2), z_lo // 4
     sibling = device_at(x, y, z, 1 - c)
-    pair = device_at(x, y, z + 1 - 2 * lax.rem(z, 2), c)
+    pair = device_at(x, y, z + 1 - 2 * b0, c)
+    two = device_at(x, y, z + 2 - 4 * b1, c)
+    four = device_at(x, y, z + 4 - 8 * b2, c)
     far = device_at(x, y, lax.rem(z + 8, 16), c)
-
-    def line(j):
-        return device_at(x, y, z_hi * 8 + lax.rem(z_lo + j, 8), c)
 
     def stride(k):
         return device_at(x, y, lax.rem(z + 2 * k, 16), c)
@@ -62,42 +63,60 @@
         cp.start()
         return cp
 
-    partners = [line(j) for j in range(1, 8)]
-    partners += [device_at(x, y, (1 - z_hi) * 8 + lax.rem(z_lo + 2 * j, 8), c) for j in range(4)]
-    partners += [plane(p) for p in range(1, 16)] + [sibling]
+    partners = [stride(k) for k in line_order] + [pair]
+    partners += [plane(p) for p in plane_order] + [sibling]
     barrier = pltpu.get_barrier_semaphore()
     for to in partners:
         pl.semaphore_signal(barrier, inc=1, device_id=to, device_id_type=MESH)
 
-    part[:, :E] = dot(fi[:, :224], wi[...], ((1,), (0,))).astype(part.dtype)
-    part[:, E:] = dot(ft[...], wt[...], ((1,), (0,))).astype(part.dtype)
+    window = pl.multiple_of(jnp.minimum(z_lo * 224 // 128 * 128, 1408), 128)
+    shift = pl.multiple_of(z_lo * 224 - window, 32)
+    wi[...] = jnp.zeros_like(wi)
+    loads = [
+        pltpu.make_async_copy(fi_hbm.at[:, pl.ds(window, 384)], fi, sl.at[0]),
+        pltpu.make_async_copy(wi_hbm, wi.at[pl.ds(shift, 224)], sl.at[1]),
+        pltpu.make_async_copy(ft_hbm.at[:, pl.ds(pl.multiple_of(z_lo * 256, 256), 256)], ft, sl.at[2]),
+        pltpu.make_async_copy(wt_hbm, wt, sl.at[3]),
+    ]
+    for cp in loads:
+        cp.start()
+    for cp in loads[:2]:
+        cp.wait()
+    part[0] = dot(fi[...], wi[...], ((1,), (0,))).reshape(2, 2, 2, 16, E)
+    for cp in loads[2:]:
+        cp.wait()
+    part[1] = dot(ft[...], wt[...], ((1,), (0,))).reshape(2, 2, 2, 16, E)
     pl.semaphore_wait(barrier, len(partners))
 
-    sends = []
-    for j in line_order:
-        rows = pl.ds(pl.multiple_of(lax.rem(z_lo + j, 8) * 16, 16), 16)
-        sends.append(send(part.at[rows], part_in.at[j - 1], s1.at[j - 1], r1.at[j - 1], line(j)))
-    pre = part[pl.ds(pl.multiple_of(z_lo * 16, 16), 16), :].astype(f32)
-    for cp in sends:
-        cp.wait()
-    for j in range(7):
-        pre = pre + part_in[j].astype(f32)
-
-    pre_i, pre_t = pre[:, :E], pre[:, E:]
+    step_1 = [send(part.at[h, :, :, 1 - b0], in_1.at[h], s1.at[h, 0], r1.at[h, 0], pair) for h in range(2)]
+    step_2, step_3 = [], []
+    for h in range(2):
+        step_1[h].wait_recv()
+        acc_1[h] = part[h, :, :, b0] + in_1[h]
+        step_2.append(send(acc_1.at[h, :, 1 - b1], in_2.at[h], s1.at[h, 1], r1.at[h, 1], two))
+    for h in range(2):
+        step_2[h].wait_recv()
+        acc_2[h] = acc_1[h, :, b1] + in_2[h]
+        step_3.append(send(acc_2.at[h, 1 - b2], in_3.at[h], s1.at[h, 2], r1.at[h, 2], four))
+
+    step_3[0].wait_recv()
+    pre_i = acc_2[0, b2] + in_3[0]
     inv_i = lax.rsqrt(jnp.sum(pre_i * pre_i, 1, keepdims=True) + norm_eps)
+    unit_i = pre_i * inv_i
+    images[0:16, :] = unit_i.astype(bf16)
+    swap = send(images.at[pl.ds(0, 16)], images.at[pl.ds(16, 16)], sx.at[0], rx.at[0], pair)
+    isends = []
+    for p in plane_order:
+        isends.append(send(images.at[pl.ds(0, 16)], images.at[pl.ds(32 * p, 16)], si.at[0, p], ri.at[0, p], plane(p)))
+    step_3[1].wait_recv()
+    pre_t = acc_2[1, b2] + in_3[1]
     inv_t = lax.rsqrt(jnp.sum(pre_t * pre_t, 1, keepdims=True) + norm_eps)
-    unit_i, unit_t = pre_i * inv_i, pre_t * inv_t
-    images[0:16, :] = unit_i.astype(bf16)
+    unit_t = pre_t * inv_t
     texts[0:16, :] = unit_t.astype(bf16)
-
-    swap = send(images.at[pl.ds(0, 16)], images.at[pl.ds(16, 16)], sx.at[0], rx.at[0], pair)
     tsends = {}
     for k in line_order:
         tsends[k] = send(texts.at[pl.ds(0, 16)], texts.at[pl.ds(16 * k, 16)], st.at[k], rt.at[k], stride(k))
     sib = [send(texts.at[pl.ds(0, 16)], texts.at[pl.ds(128, 16)], ss.at[0], rs.at[0], sibling)]
-    isends = []
-    for p in plane_order:
-        isends.append(send(images.at[pl.ds(0, 16)], images.at[pl.ds(32 * p, 16)], si.at[0, p], ri.at[0, p], plane(p)))
     swap.wait()
     for p in plane_order:
         isends.append(send(images.at[pl.ds(16, 16)], images.at[pl.ds(32 * p + 16, 16)], si.at[1, p], ri.at[1, p], plane(p)))
@@ -106,6 +125,8 @@
         sib.append(send(texts.at[pl.ds(16 * k, 16)], texts.at[pl.ds(128 + 16 * k, 16)], ss.at[k], rs.at[k], sibling))
     for cp in sib + isends:
         cp.wait()
+    for cp in step_1 + step_2 + step_3:
+        cp.wait_send()
 
     scale = jnp.exp(jnp.full((8, 128), ls[0], f32))[0:1, 0:1]
     bias = lb[0]
@@ -144,28 +165,39 @@
         sum_i = sum_i + dz_i_in[p].astype(f32)
     swap_out[...] = sum_i[16:32, :]
     swap = send(swap_out, swap_in, sx.at[1], rx.at[1], pair)
+    swap.wait()
+    sum_i = sum_i[0:16, :] + swap_in[...]
+    dots_i = jnp.sum(sum_i * unit_i, 1, keepdims=True)
+    back[0, b2, b1, b0] = (inv_i * (sum_i - unit_i * dots_i)).astype(bf16)
+
+    def spread(h, step):
+        block = (
+            back.at[h, b2, b1, b0] if step == 0 else back.at[h, :, b1, b0] if step == 1 else back.at[h, :, :, b0]
+        )
+        return send(block, block, sb.at[h, step], rb.at[h, step], (four, two, pair)[step])
+
+    spreads = [spread(0, 0)]
     sum_t = dz_text[0:16, :]
     for cp in dtsends:
         cp.wait()
     for k in range(1, 8):
         sum_t = sum_t + dz_t_in[k].astype(f32)
-    swap.wait()
-    sum_i = sum_i[0:16, :] + swap_in[...]
-
-    dots_i = jnp.sum(sum_i * unit_i, 1, keepdims=True)
     dots_t = jnp.sum(sum_t * unit_t, 1, keepdims=True)
-    own = pl.ds(pl.multiple_of(z_lo * 16, 16), 16)
-    back_i[own, :] = (inv_i * (sum_i - unit_i * dots_i)).astype(bf16)
-    back_t[own, :] = (inv_t * (sum_t - unit_t * dots_t)).astype(bf16)
-    bsends = []
-    for j in line_order:
-        bsends.append(send(back_i.at[own], back_i.at[own], sb.at[0, j - 1], rb.at[0, j - 1], line(j)))
-        bsends.append(send(back_t.at[own], back_t.at[own], sb.at[1, j - 1], rb.at[1, j - 1], line(j)))
-    for cp in bsends:
-        cp.wait()
-
-    grads[0:8] = dot(fi[...], back_i[...], ((0,), (0,))).reshape(8, 32, E)
-    grads[8:16] = dot(ft[...], back_t[...], ((0,), (0,))).reshape(8, 32, E)
+    back[1, b2, b1, b0] = (inv_t * (sum_t - unit_t * dots_t)).astype(bf16)
+    spreads.append(spread(1, 0))
+    for step in (1, 2):
+        for h in range(2):
+            spreads[-2].wait_recv()
+            spreads.append(spread(h, step))
+    spreads[4].wait_recv()
+    grad_i[...] = dot(fi[...], back[0].reshape(128, E), ((0,), (0,)))
+    for t in range(7):
+        grads[t] = grad_i[pl.ds(pl.multiple_of(shift + 32 * t, 32), 32), :]
+    grads[7] = jnp.zeros((32, E), f32)
+    spreads[5].wait_recv()
+    grads[8:16] = dot(ft[...], back[1].reshape(128, E), ((0,), (0,))).reshape(8, 32, E)
+    for cp in spreads:
+        cp.wait_send()
     give = pl.ds(pl.multiple_of((1 - c) * 16, 16), 16)
     keep = pl.ds(pl.multiple_of(c * 16, 16), 16)
     gsib = send(grads.at[:, give], grads_sib_in, sm.at[0], rm.at[0], sibling)
@@ -201,37 +233,36 @@
 
 
 def on_device(image_feats, text_feats, image_proj, text_proj, log_scale, logit_bias):
-    m = lax.axis_index("mp")
-    fi = jnp.pad(lax.dynamic_slice_in_dim(image_feats, m * 224, 224, 1), ((0, 0), (0, 32)))
-    ft = lax.dynamic_slice_in_dim(text_feats, m * 256, 256, 1)
     dma = pltpu.SemaphoreType.DMA
     vmem = pltpu.VMEM
-    wire_1, wire_dz, wire_g, wire_o = f32, bf16, bf16, bf16
+    wire_dz, wire_g, wire_o = bf16, bf16, bf16
     grads = pl.pallas_call(
         kernel,
         out_shape=jax.ShapeDtypeStruct((512, E), wire_o),
-        in_specs=[pl.BlockSpec(memory_space=vmem)] * 4 + [pl.BlockSpec(memory_space=pltpu.SMEM)] * 2,
+        in_specs=[pl.BlockSpec(memory_space=pl.ANY)] * 4 + [pl.BlockSpec(memory_space=pltpu.SMEM)] * 2,
         out_specs=pl.BlockSpec(memory_space=vmem),
         scratch_shapes=[
-            vmem((128, 2 * E), wire_1), vmem((7, 16, 2 * E), wire_1),
+            vmem((128, 384), bf16), vmem((128, 256), bf16), vmem((384, E), bf16), vmem((256, E), bf16),
+            vmem((2, 2, 2, 2, 16, E), f32), vmem((2, 2, 2, 16, E), f32), vmem((2, 2, 16, E), f32),
+            vmem((2, 2, 2, 16, E), f32), vmem((2, 2, 16, E), f32), vmem((2, 16, E), f32),
             vmem((512, E), bf16), vmem((256, E), bf16),
             vmem((512, E), f32), vmem((256, E), f32),
             vmem((512, E), wire_dz), vmem((16, 32, E), wire_dz),
             vmem((16, E), f32), vmem((16, E), f32),
             vmem((128, E), f32), vmem((128, E), wire_dz), vmem((8, 16, E), wire_dz),
-            vmem((128, E), bf16), vmem((128, E), bf16),
+            vmem((2, 2, 2, 2, 16, E), bf16), vmem((384, E), f32),
             vmem((16, 32, E), f32), vmem((16, 16, E), f32), vmem((16, 16, E), wire_g),
             vmem((16, 16, E), wire_g), vmem((16, E), f32), vmem((16, E), f32),
             vmem((16, 2, 16, E), wire_o),
-            dma((7,)), dma((7,)), dma((8,)), dma((8,)), dma((2,)), dma((2,)), dma((9,)), dma((9,)),
+            dma((4,)), dma((2, 3)), dma((2, 3)), dma((8,)), dma((8,)), dma((2,)), dma((2,)), dma((9,)), dma((9,)),
             dma((2, 16)), dma((2, 16)), dma((16,)), dma((16,)), dma((8,)), dma((8,)),
-            dma((2, 7)), dma((2, 7)), dma((16,)), dma((16,)), dma((16,)), dma((16,)), dma((3,)), dma((3,)),
+            dma((2, 3)), dma((2, 3)), dma((16,)), dma((16,)), dma((16,)), dma((16,)), dma((3,)), dma((3,)),
         ],
         compiler_params=pltpu.CompilerParams(
             collective_id=0, has_side_effects=True, vmem_limit_bytes=48 * 2**20
         ),
         name="heads",
-    )(fi, ft, image_proj, text_proj, log_scale, logit_bias)
+    )(image_feats, text_feats, image_proj, text_proj, log_scale, logit_bias)
     return grads[:224].astype(f32), grads[256:].astype(f32)
 
 

time: 180 us -> 158 us (0.88)
  the two profiles are of different devices: /device:TPU:97 before, /device:TPU:1 now
where the time goes in v2:
time: 158 us; the launch traced here: 157 us
  Pallas kernels  149 us (94%)
  local copies, waits for them, and re-layouts  4.15 us (3%)
  other arithmetic  2.12 us (1%)
  between operations  1.94 us (1%)
    pallas_call x1, Pallas kernels, on_device(): pl.pallas_call(kernel, out_shape=jax.ShapeDtypeStruct((512, E), wire_o),...  149 us
    unnamed x8, local copies, waits for them, and re-layouts  4.15 us

profile of v2, /device:TPU:1, one launch (start us, length us, event | category | flops | bytes accessed | tf_op | source)
XLA Modules:
  0.0 157.3 jit_solution(17465714017528586431)
XLA Ops:
  1.9 0.0 copy-start
  1.9 1.1 copy-done
  3.0 0.0 copy-start.1
  3.0 1.0 copy-done.1
  4.0 0.0 copy-start.2
  4.0 1.0 copy-done.2
  5.1 0.0 copy-start.3
  5.1 1.0 copy-done.3
  6.1 149.1 %heads.1 = bf16[512,1152]{1,0:T(8,128)(2,1)S(1)} custom-call(bf16[128,1792]{1,0:T(8,128)(2,1)S(1)} %copy-done.3, bf16[128,2048]{1,0:T(8,128)(2,1)S(1)} %copy-done.1, bf16[224,1152]{1,0:T(8,128)(2,1)S(1)} %copy-done.2, bf16[256,1152]{1,0:T(8,128)(2,1)S(1)} %copy-done, f32[1]{0:T(128)S(6)} %copy.8.ls, f32[1]{0:T(128)S(6)} %copy.9.lb), custom_call_target="tpu_custom_call" | custom-call | tf_op jit(solution)/shard_map/heads/pallas_call | solution.py:239
  155.2 1.0 slice_convert_fusion.1
  156.2 1.1 slice_convert_fusion
Async XLA Ops:
  1.9 1.1 copy-start
  3.0 1.0 copy-start.1
  4.0 1.0 copy-start.2
  5.1 1.0 copy-start.3

commit v3 on v2

--- a/solution.py
+++ b/solution.py
@@ -25,7 +25,7 @@
 
 def kernel(
     fi_hbm, ft_hbm, wi_hbm, wt_hbm, ls, lb, out,
-    fi, ft, wi, wt, part, acc_1, acc_2, in_1, in_2, in_3,
+    fi, ft, wi, wt, part, part_w, acc_1, acc_1w, acc_2, in_1, in_2, in_3,
     images, texts, dz_i, dz_t, dz_i_wire, dz_i_in, swap_out, swap_in,
     text_sib_in, dz_t_wire, dz_t_in, back, grad_i, grads, grads_sib_in, grads_wire,
     grads_in, zsum_out, zsum_in, result,
@@ -83,20 +83,23 @@
     for cp in loads[:2]:
         cp.wait()
     part[0] = dot(fi[...], wi[...], ((1,), (0,))).reshape(2, 2, 2, 16, E)
+    part_w[0] = part[0].astype(bf16)
     for cp in loads[2:]:
         cp.wait()
     part[1] = dot(ft[...], wt[...], ((1,), (0,))).reshape(2, 2, 2, 16, E)
+    part_w[1] = part[1].astype(bf16)
     pl.semaphore_wait(barrier, len(partners))
 
-    step_1 = [send(part.at[h, :, :, 1 - b0], in_1.at[h], s1.at[h, 0], r1.at[h, 0], pair) for h in range(2)]
+    step_1 = [send(part_w.at[h, :, :, 1 - b0], in_1.at[h], s1.at[h, 0], r1.at[h, 0], pair) for h in range(2)]
     step_2, step_3 = [], []
     for h in range(2):
         step_1[h].wait_recv()
-        acc_1[h] = part[h, :, :, b0] + in_1[h]
-        step_2.append(send(acc_1.at[h, :, 1 - b1], in_2.at[h], s1.at[h, 1], r1.at[h, 1], two))
+        acc_1[h] = part[h, :, :, b0] + in_1[h].astype(f32)
+        acc_1w[h] = acc_1[h].astype(bf16)
+        step_2.append(send(acc_1w.at[h, :, 1 - b1], in_2.at[h], s1.at[h, 1], r1.at[h, 1], two))
     for h in range(2):
         step_2[h].wait_recv()
-        acc_2[h] = acc_1[h, :, b1] + in_2[h]
+        acc_2[h] = acc_1[h, :, b1] + in_2[h].astype(f32)
         step_3.append(send(acc_2.at[h, 1 - b2], in_3.at[h], s1.at[h, 2], r1.at[h, 2], four))
 
     step_3[0].wait_recv()
@@ -130,28 +133,32 @@
 
     scale = jnp.exp(jnp.full((8, 128), ls[0], f32))[0:1, 0:1]
     bias = lb[0]
-    dz_t[...] = jnp.zeros_like(dz_t)
-
-    def chunk(i, carry):
-        rows = pl.ds(pl.multiple_of(i * 128, 128), 128)
+
+    dsends = []
+    for i in (2, 1, 3, 0):
+        rows = slice(i * 128, i * 128 + 128)
         mine, every = images[rows, :], texts[...]
         logits = scale * dot(mine, every, ((1,), (1,))) + bias
-        row = lax.broadcasted_iota(jnp.int32, (128, 256), 0) + i * 128
-        col = lax.broadcasted_iota(jnp.int32, (128, 256), 1)
-        matched = (row == col) & (row < 16)
-        sig = jax.nn.sigmoid(jnp.where(matched, -logits, logits))
-        weights = (scale * jnp.where(matched, -sig, sig)).astype(bf16)
-        dz_i[rows, :] = dot(weights, every, ((1,), (0,)))
-        dz_t[...] += dot(weights, mine, ((0,), (0,)))
-        return carry
-
-    lax.fori_loop(0, 4, chunk, 0)
+        if i == 0:
+            row = lax.broadcasted_iota(jnp.int32, (128, 256), 0)
+            col = lax.broadcasted_iota(jnp.int32, (128, 256), 1)
+            matched = (row == col) & (row < 16)
+            sig = jax.nn.sigmoid(jnp.where(matched, -logits, logits))
+            slopes = jnp.where(matched, -sig, sig)
+        else:
+            slopes = jax.nn.sigmoid(logits)
+        weights = (scale * slopes).astype(bf16)
+        dz_rows = dot(weights, every, ((1,), (0,)))
+        if i == 0:
+            dz_i[...] = dz_rows[0:32]
+        dz_i_wire[rows, :] = dz_rows.astype(dz_i_wire.dtype)
+        for p in plane_order:
+            if p // 4 == i:
+                dsends.append(send(dz_i_wire.at[pl.ds(32 * p, 32)], dz_i_in.at[p], sdi.at[p], rdi.at[p], plane_back(p)))
+        more = dot(weights, mine, ((0,), (0,)))
+        dz_t[...] = more if i == 2 else dz_t[...] + more
 
     tsib = send(dz_t.at[pl.ds(128, 128)], text_sib_in, ss.at[8], rs.at[8], sibling)
-    dz_i_wire[...] = dz_i[...].astype(dz_i_wire.dtype)
-    dsends = []
-    for p in plane_order:
-        dsends.append(send(dz_i_wire.at[pl.ds(32 * p, 32)], dz_i_in.at[p], sdi.at[p], rdi.at[p], plane_back(p)))
     tsib.wait()
     dz_text = dz_t[0:128, :] + text_sib_in[...]
     dz_t_wire[...] = dz_text.astype(dz_t_wire.dtype)
@@ -190,45 +197,59 @@
             spreads[-2].wait_recv()
             spreads.append(spread(h, step))
     spreads[4].wait_recv()
+    give = pl.ds(pl.multiple_of((1 - c) * 16, 16), 16)
+    keep = pl.ds(pl.multiple_of(c * 16, 16), 16)
+    halves = (pl.ds(0, 8), pl.ds(8, 8))
     grad_i[...] = dot(fi[...], back[0].reshape(128, E), ((0,), (0,)))
     for t in range(7):
         grads[t] = grad_i[pl.ds(pl.multiple_of(shift + 32 * t, 32), 32), :]
     grads[7] = jnp.zeros((32, E), f32)
+    gsib = [send(grads.at[halves[0], give], grads_sib_in.at[halves[0]], sm.at[0], rm.at[0], sibling)]
     spreads[5].wait_recv()
     grads[8:16] = dot(ft[...], back[1].reshape(128, E), ((0,), (0,))).reshape(8, 32, E)
+    gsib.append(send(grads.at[halves[1], give], grads_sib_in.at[halves[1]], sm.at[1], rm.at[1], sibling))
     for cp in spreads:
         cp.wait_send()
-    give = pl.ds(pl.multiple_of((1 - c) * 16, 16), 16)
-    keep = pl.ds(pl.multiple_of(c * 16, 16), 16)
-    gsib = send(grads.at[:, give], grads_sib_in, sm.at[0], rm.at[0], sibling)
-    gsib.wait()
-    me = plane_index(0)
 
     def add_tile(t, carry):
         grads_wire[t] = (grads[t, keep, :] + grads_sib_in[t]).astype(grads_wire.dtype)
         return carry
 
-    lax.fori_loop(0, 16, add_tile, 0)
-    gsends = []
-    for p in plane_order:
-        gsends.append(send(grads_wire.at[plane_index(p)], grads_in.at[p], sg.at[p], rg.at[p], plane(p)))
-    total = grads[me, keep, :] + grads_sib_in[me]
-    for cp in gsends:
-        cp.wait()
-    for p in range(1, 16):
-        total = total + grads_in[p].astype(f32)
-    zsum_out[...] = total
-    zs = send(zsum_out, zsum_in, sm.at[1], rm.at[1], far)
-    zs.wait()
-    result[me, c] = (total + zsum_in[...]).astype(result.dtype)
-    tile = result.at[me, c]
-    osends = []
-    for p in plane_order:
-        osends.append(send(tile, tile, so.at[p], ro.at[p], plane(p)))
-    for cp in osends:
-        cp.wait()
-    whole = send(result.at[:, c], result.at[:, c], sm.at[2], rm.at[2], sibling)
-    whole.wait()
+    for h in range(2):
+        gsib[h].wait()
+        lax.fori_loop(8 * h, 8 * h + 8, add_tile, 0)
+    me = plane_index(0)
+    runs = (slice(0, 640), slice(640, E))
+    spans = (pl.ds(0, 640), pl.ds(640, 512))
+    gsends, zsends, osends, totals = [], [], [], []
+    for h, cols in enumerate(spans):
+        gsends.append([
+            send(grads_wire.at[plane_index(p), :, cols], grads_in.at[p, :, cols], sg.at[h, p], rg.at[h, p], plane(p))
+            for p in plane_order
+        ])
+    for h, run in enumerate(runs):
+        total = grads[me, keep, run] + grads_sib_in[me, :, run]
+        for cp in gsends[h]:
+            cp.wait_recv()
+        for p in range(1, 16):
+            total = total + grads_in[p, :, run].astype(f32)
+        zsum_out[:, run] = total
+        zsends.append(send(zsum_out.at[:, spans[h]], zsum_in.at[:, spans[h]], sm.at[2 + h], rm.at[2 + h], far))
+    for h, run in enumerate(runs):
+        zsends[h].wait_recv()
+        result[me, c, :, run] = (zsum_out[:, run] + zsum_in[:, run]).astype(result.dtype)
+        tile = result.at[me, c, :, spans[h]]
+        osends.append([send(tile, tile, so.at[h, p], ro.at[h, p], plane(p)) for p in plane_order])
+    whole = []
+    for h in range(2):
+        for cp in osends[h]:
+            cp.wait_recv()
+        block = result.at[:, c, :, spans[h]]
+        whole.append(send(block, block, sm.at[4 + h], rm.at[4 + h], sibling))
+    for cp in gsends[0] + gsends[1] + zsends + osends[0] + osends[1]:
+        cp.wait_send()
+    for cp in whole:
+        cp.wait()
     out[...] = result[...].reshape(512, E)
 
 
@@ -243,10 +264,12 @@
         out_specs=pl.BlockSpec(memory_space=vmem),
         scratch_shapes=[
             vmem((128, 384), bf16), vmem((128, 256), bf16), vmem((384, E), bf16), vmem((256, E), bf16),
-            vmem((2, 2, 2, 2, 16, E), f32), vmem((2, 2, 2, 16, E), f32), vmem((2, 2, 16, E), f32),
-            vmem((2, 2, 2, 16, E), f32), vmem((2, 2, 16, E), f32), vmem((2, 16, E), f32),
+            vmem((2, 2, 2, 2, 16, E), f32), vmem((2, 2, 2, 2, 16, E), bf16),
+            vmem((2, 2, 2, 16, E), f32), vmem((2, 2, 2, 16, E), bf16),
+            vmem((2, 2, 16, E), f32),
+            vmem((2, 2, 2, 16, E), bf16), vmem((2, 2, 16, E), bf16), vmem((2, 16, E), f32),
             vmem((512, E), bf16), vmem((256, E), bf16),
-            vmem((512, E), f32), vmem((256, E), f32),
+            vmem((32, E), f32), vmem((256, E), f32),
             vmem((512, E), wire_dz), vmem((16, 32, E), wire_dz),
             vmem((16, E), f32), vmem((16, E), f32),
             vmem((128, E), f32), vmem((128, E), wire_dz), vmem((8, 16, E), wire_dz),
@@ -256,10 +279,10 @@
             vmem((16, 2, 16, E), wire_o),
             dma((4,)), dma((2, 3)), dma((2, 3)), dma((8,)), dma((8,)), dma((2,)), dma((2,)), dma((9,)), dma((9,)),
             dma((2, 16)), dma((2, 16)), dma((16,)), dma((16,)), dma((8,)), dma((8,)),
-            dma((2, 3)), dma((2, 3)), dma((16,)), dma((16,)), dma((16,)), dma((16,)), dma((3,)), dma((3,)),
+            dma((2, 3)), dma((2, 3)), dma((2, 16)), dma((2, 16)), dma((2, 16)), dma((2, 16)), dma((6,)), dma((6,)),
         ],
         compiler_params=pltpu.CompilerParams(
-            collective_id=0, has_side_effects=True, vmem_limit_bytes=48 * 2**20
+            collective_id=0, has_side_effects=True, vmem_limit_bytes=62 * 2**20
         ),
         name="heads",
     )(image_feats, text_feats, image_proj, text_proj, log_scale, logit_bias)

time: 158 us -> 141 us (0.89)
  Pallas kernels: 149 us -> 136 us
  local copies, waits for them, and re-layouts: 4.15 us -> 0.01 us
    pallas_call x1, Pallas kernels: 149 us -> 136 us  [on_device(): pl.pallas_call(kernel, out_shape=jax.ShapeDtypeStruct((512, E), wire_o),...]
    unnamed x8 -> x2, local copies, waits for them, and re-layouts: 4.15 us -> 0.01 us
where the time goes in v3:
time: 141 us
  Pallas kernels  136 us (96%)
  other arithmetic  3.25 us (2%)
  between operations  1.94 us (1%)
    pallas_call x1, Pallas kernels, on_device(): pl.pallas_call(kernel, out_shape=jax.ShapeDtypeStruct((512, E), wire_o),...  136 us
    convert_element_type x2, other arithmetic, on_device(): return (grads[:224].astype(f32), grads[256:].astype(f32))  3.25 us

profile of v3, /device:TPU:1, one launch (start us, length us, event | category | flops | bytes accessed | tf_op | source)
XLA Modules:
  0.0 141.1 jit_solution(12144962194310744617)
XLA Ops:
  1.9 135.9 %heads.1 = bf16[512,1152]{1,0:T(8,128)(2,1)} custom-call(bf16[128,1792]{1,0:T(8,128)(2,1)} %fi_hbm.1, bf16[128,2048]{1,0:T(8,128)(2,1)} %ft_hbm.1, bf16[224,1152]{1,0:T(8,128)(2,1)} %wi_hbm.1, bf16[256,1152]{1,0:T(8,128)(2,1)} %wt_hbm.1, f32[1]{0:T(128)S(6)} %copy.8.ls, f32[1]{0:T(128)S(6)} %copy.9.lb), custom_call_target="tpu_custom_call" | custom-call | tf_op jit(solution)/shard_map/heads/pallas_call | solution.py:260
  137.8 0.0 copy-start
  137.8 2.2 %slice_convert_fusion.1 = f32[224,1152]{1,0:T(8,128)} fusion(bf16[512,1152]{1,0:T(8,128)(2,1)} %heads.1), kind=kLoop, calls=%fused_computation.1 | loop fusion | flops 258048 | bytes 1548288 | tf_op jit(solution)/shard_map/convert_element_type | solution.py:289
  140.0 0.0 copy-done
  140.0 1.1 slice_convert_fusion
Async XLA Ops:
  137.8 2.2 %copy-start = (bf16[512,1152]{1,0:T(8,128)(2,1)S(1)}, bf16[512,1152]{1,0:T(8,128)(2,1)}, u32[]{:S(2)}) copy-start(bf16[512,1152]{1,0:T(8,128)(2,1)} %heads.1) | copy-start | bytes 3538948

commit v4 on v3

--- a/solution.py
+++ b/solution.py
@@ -28,8 +28,8 @@
     fi, ft, wi, wt, part, part_w, acc_1, acc_1w, acc_2, in_1, in_2, in_3,
     images, texts, dz_i, dz_t, dz_i_wire, dz_i_in, swap_out, swap_in,
     text_sib_in, dz_t_wire, dz_t_in, back, grad_i, grads, grads_sib_in, grads_wire,
-    grads_in, zsum_out, zsum_in, result,
-    sl, s1, r1, st, rt, sx, rx, ss, rs, si, ri, sdi, rdi, sdt, rdt, sb, rb, sg, rg, so, ro, sm, rm,
+    grads_in, zsum_out, zsum_in,
+    sl, s1, r1, st, rt, sx, rx, ss, rs, si, ri, sdi, rdi, sdt, rdt, sb, rb, sg, rg, so, ro, sm, rm, gate,
 ):
     d, z_lo = lax.axis_index("dp"), lax.axis_index("mp")
     c, x, y, z_hi = lax.rem(d, 2), lax.rem(d // 2, 4), lax.rem(d // 8, 4), d // 32
@@ -63,11 +63,21 @@
         cp.start()
         return cp
 
-    partners = [stride(k) for k in line_order] + [pair]
-    partners += [plane(p) for p in plane_order] + [sibling]
+    def along(k):
+        return device_at(x, y, lax.rem(z + 16 + k, 16), c)
+
+    partners = [along(1), along(-1)] + [plane(p) for p in plane_order] + [sibling]
     barrier = pltpu.get_barrier_semaphore()
     for to in partners:
         pl.semaphore_signal(barrier, inc=1, device_id=to, device_id_type=MESH)
+
+    def greet(r):
+        pl.semaphore_signal(gate.at[r, 0], inc=1, device_id=along(2**r), device_id_type=MESH)
+        pl.semaphore_signal(gate.at[r, 1], inc=1, device_id=along(-(2**r)), device_id_type=MESH)
+
+    def greeted(r):
+        pl.semaphore_wait(gate.at[r, 0], 1)
+        pl.semaphore_wait(gate.at[r, 1], 1)
 
     window = pl.multiple_of(jnp.minimum(z_lo * 224 // 128 * 128, 1408), 128)
     shift = pl.multiple_of(z_lo * 224 - window, 32)
@@ -89,14 +99,19 @@
     part[1] = dot(ft[...], wt[...], ((1,), (0,))).reshape(2, 2, 2, 16, E)
     part_w[1] = part[1].astype(bf16)
     pl.semaphore_wait(barrier, len(partners))
+    greet(0)
 
     step_1 = [send(part_w.at[h, :, :, 1 - b0], in_1.at[h], s1.at[h, 0], r1.at[h, 0], pair) for h in range(2)]
+    greeted(0)
+    greet(1)
     step_2, step_3 = [], []
     for h in range(2):
         step_1[h].wait_recv()
         acc_1[h] = part[h, :, :, b0] + in_1[h].astype(f32)
         acc_1w[h] = acc_1[h].astype(bf16)
         step_2.append(send(acc_1w.at[h, :, 1 - b1], in_2.at[h], s1.at[h, 1], r1.at[h, 1], two))
+    greeted(1)
+    greet(2)
     for h in range(2):
         step_2[h].wait_recv()
         acc_2[h] = acc_1[h, :, b1] + in_2[h].astype(f32)
@@ -116,6 +131,7 @@
     inv_t = lax.rsqrt(jnp.sum(pre_t * pre_t, 1, keepdims=True) + norm_eps)
     unit_t = pre_t * inv_t
     texts[0:16, :] = unit_t.astype(bf16)
+    greeted(2)
     tsends = {}
     for k in line_order:
         tsends[k] = send(texts.at[pl.ds(0, 16)], texts.at[pl.ds(16 * k, 16)], st.at[k], rt.at[k], stride(k))
@@ -237,20 +253,19 @@
         zsends.append(send(zsum_out.at[:, spans[h]], zsum_in.at[:, spans[h]], sm.at[2 + h], rm.at[2 + h], far))
     for h, run in enumerate(runs):
         zsends[h].wait_recv()
-        result[me, c, :, run] = (zsum_out[:, run] + zsum_in[:, run]).astype(result.dtype)
-        tile = result.at[me, c, :, spans[h]]
+        out[me, c, :, run] = (zsum_out[:, run] + zsum_in[:, run]).astype(out.dtype)
+        tile = out.at[me, c, :, spans[h]]
         osends.append([send(tile, tile, so.at[h, p], ro.at[h, p], plane(p)) for p in plane_order])
     whole = []
     for h in range(2):
         for cp in osends[h]:
             cp.wait_recv()
-        block = result.at[:, c, :, spans[h]]
+        block = out.at[:, c, :, spans[h]]
         whole.append(send(block, block, sm.at[4 + h], rm.at[4 + h], sibling))
     for cp in gsends[0] + gsends[1] + zsends + osends[0] + osends[1]:
         cp.wait_send()
     for cp in whole:
         cp.wait()
-    out[...] = result[...].reshape(512, E)
 
 
 def on_device(image_feats, text_feats, image_proj, text_proj, log_scale, logit_bias):
@@ -259,7 +274,7 @@
     wire_dz, wire_g, wire_o = bf16, bf16, bf16
     grads = pl.pallas_call(
         kernel,
-        out_shape=jax.ShapeDtypeStruct((512, E), wire_o),
+        out_shape=jax.ShapeDtypeStruct((16, 2, 16, E), wire_o),
         in_specs=[pl.BlockSpec(memory_space=pl.ANY)] * 4 + [pl.BlockSpec(memory_space=pltpu.SMEM)] * 2,
         out_specs=pl.BlockSpec(memory_space=vmem),
         scratch_shapes=[
@@ -276,16 +291,16 @@
             vmem((2, 2, 2, 2, 16, E), bf16), vmem((384, E), f32),
             vmem((16, 32, E), f32), vmem((16, 16, E), f32), vmem((16, 16, E), wire_g),
             vmem((16, 16, E), wire_g), vmem((16, E), f32), vmem((16, E), f32),
-            vmem((16, 2, 16, E), wire_o),
             dma((4,)), dma((2, 3)), dma((2, 3)), dma((8,)), dma((8,)), dma((2,)), dma((2,)), dma((9,)), dma((9,)),
             dma((2, 16)), dma((2, 16)), dma((16,)), dma((16,)), dma((8,)), dma((8,)),
-            dma((2, 3)), dma((2, 3)), dma((2, 16)), dma((2, 16)), dma((2, 16)), dma((2, 16)), dma((6,)), dma((6,)),
+            dma((2, 3)), dma((2, 3)), dma((2, 16)), dma((2, 16)), dma((2, 16)), dma((2, 16)), dma((6,)), dma((6,)), pltpu.SemaphoreType.REGULAR((3, 2)),
         ],
         compiler_params=pltpu.CompilerParams(
             collective_id=0, has_side_effects=True, vmem_limit_bytes=62 * 2**20
         ),
         name="heads",
     )(image_feats, text_feats, image_proj, text_proj, log_scale, logit_bias)
+    grads = grads.reshape(512, E)
     return grads[:224].astype(f32), grads[256:].astype(f32)
 
 

time: 141 us -> 140 us (level)
  Pallas kernels: 136 us -> 134 us
    pallas_call x1, Pallas kernels: 136 us -> 134 us  [on_device(): pl.pallas_call(kernel, out_shape=jax.ShapeDtypeStruct((16, 2, 16, E), wir...]
where the time goes in v4:
time: 140 us; the launch traced here: 139 us
  Pallas kernels  134 us (96%)
  other arithmetic  2.2 us (2%)
  between operations  1.95 us (1%)
    pallas_call x1, Pallas kernels, on_device(): pl.pallas_call(kernel, out_shape=jax.ShapeDtypeStruct((16, 2, 16, E), wir...  134 us

profile of v4, /device:TPU:1, one launch (start us, length us, event | category | flops | bytes accessed | tf_op | source)
XLA Modules:
  0.0 139.4 jit_solution(2030678421622846329)
XLA Ops:
  1.9 134.3 %heads.1 = bf16[16,2,16,1152]{3,2,1,0:T(8,128)(2,1)} custom-call(bf16[128,1792]{1,0:T(8,128)(2,1)} %fi_hbm.1, bf16[128,2048]{1,0:T(8,128)(2,1)} %ft_hbm.1, bf16[224,1152]{1,0:T(8,128)(2,1)} %wi_hbm.1, bf16[256,1152]{1,0:T(8,128)(2,1)} %wt_hbm.1, f32[1]{0:T(128)S(6)} %copy.8.ls, f32[1]{0:T(128)S(6)} %copy.9.lb), custom_call_target="tpu_custom_call" | custom-call | tf_op jit(solution)/shard_map/heads/pallas_call | solution.py:275
  136.2 0.0 slice-start
  136.2 0.0 slice-start.1
  136.2 1.0 slice-done
  137.2 1.1 bitcast_convert_fusion.1
  138.3 0.0 slice-done.1
  138.3 1.1 bitcast_convert_fusion
Async XLA Ops:
  136.2 1.0 slice-start
  136.2 2.1 %slice-start.1 = ((bf16[16,2,16,1152]{3,2,1,0:T(8,128)(2,1)}), bf16[8,2,16,1152]{3,2,1,0:T(8,128)(2,1)S(1)}, s32[]{:S(2)}) async-start(bf16[16,2,16,1152]{3,2,1,0:T(8,128)(2,1)} %heads.1), calls=%async_computation.1 | async-start | bytes 1179648 | tf_op jit(solution)/shard_map/slice | solution.py:304

commit v5 on v4

--- a/solution.py
+++ b/solution.py
@@ -25,7 +25,7 @@
 
 def kernel(
     fi_hbm, ft_hbm, wi_hbm, wt_hbm, ls, lb, out,
-    fi, ft, wi, wt, part, part_w, acc_1, acc_1w, acc_2, in_1, in_2, in_3,
+    fi, ft, wi, wt, part, part_w, acc_1, acc_1w, acc_2, acc_2w, in_1, in_2, in_3,
     images, texts, dz_i, dz_t, dz_i_wire, dz_i_in, swap_out, swap_in,
     text_sib_in, dz_t_wire, dz_t_in, back, grad_i, grads, grads_sib_in, grads_wire,
     grads_in, zsum_out, zsum_in,
@@ -115,10 +115,11 @@
     for h in range(2):
         step_2[h].wait_recv()
         acc_2[h] = acc_1[h, :, b1] + in_2[h].astype(f32)
-        step_3.append(send(acc_2.at[h, 1 - b2], in_3.at[h], s1.at[h, 2], r1.at[h, 2], four))
+        acc_2w[h] = acc_2[h].astype(bf16)
+        step_3.append(send(acc_2w.at[h, 1 - b2], in_3.at[h], s1.at[h, 2], r1.at[h, 2], four))
 
     step_3[0].wait_recv()
-    pre_i = acc_2[0, b2] + in_3[0]
+    pre_i = acc_2[0, b2] + in_3[0].astype(f32)
     inv_i = lax.rsqrt(jnp.sum(pre_i * pre_i, 1, keepdims=True) + norm_eps)
     unit_i = pre_i * inv_i
     images[0:16, :] = unit_i.astype(bf16)
@@ -127,7 +128,7 @@
     for p in plane_order:
         isends.append(send(images.at[pl.ds(0, 16)], images.at[pl.ds(32 * p, 16)], si.at[0, p], ri.at[0, p], plane(p)))
     step_3[1].wait_recv()
-    pre_t = acc_2[1, b2] + in_3[1]
+    pre_t = acc_2[1, b2] + in_3[1].astype(f32)
     inv_t = lax.rsqrt(jnp.sum(pre_t * pre_t, 1, keepdims=True) + norm_eps)
     unit_t = pre_t * inv_t
     texts[0:16, :] = unit_t.astype(bf16)
@@ -271,7 +272,7 @@
 def on_device(image_feats, text_feats, image_proj, text_proj, log_scale, logit_bias):
     dma = pltpu.SemaphoreType.DMA
     vmem = pltpu.VMEM
-    wire_dz, wire_g, wire_o = bf16, bf16, bf16
+    wire_dz, wire_g, wire_o = bf16, f32, bf16
     grads = pl.pallas_call(
         kernel,
         out_shape=jax.ShapeDtypeStruct((16, 2, 16, E), wire_o),
@@ -281,8 +282,8 @@
             vmem((128, 384), bf16), vmem((128, 256), bf16), vmem((384, E), bf16), vmem((256, E), bf16),
             vmem((2, 2, 2, 2, 16, E), f32), vmem((2, 2, 2, 2, 16, E), bf16),
             vmem((2, 2, 2, 16, E), f32), vmem((2, 2, 2, 16, E), bf16),
-            vmem((2, 2, 16, E), f32),
-            vmem((2, 2, 2, 16, E), bf16), vmem((2, 2, 16, E), bf16), vmem((2, 16, E), f32),
+            vmem((2, 2, 16, E), f32), vmem((2, 2, 16, E), bf16),
+            vmem((2, 2, 2, 16, E), bf16), vmem((2, 2, 16, E), bf16), vmem((2, 16, E), bf16),
             vmem((512, E), bf16), vmem((256, E), bf16),
             vmem((32, E), f32), vmem((256, E), f32),
             vmem((512, E), wire_dz), vmem((16, 32, E), wire_dz),

time: 140 us -> 137 us (0.979)
  Pallas kernels: 134 us -> 132 us
    pallas_call x1, Pallas kernels: 134 us -> 132 us  [on_device(): pl.pallas_call(kernel, out_shape=jax.ShapeDtypeStruct((16, 2, 16, E), wir...]
where the time goes in v5:
time: 137 us
  Pallas kernels  132 us (96%)
  other arithmetic  2.2 us (2%)
  between operations  1.95 us (1%)
    pallas_call x1, Pallas kernels, on_device(): pl.pallas_call(kernel, out_shape=jax.ShapeDtypeStruct((16, 2, 16, E), wir...  132 us

profile of v5, /device:TPU:1, one launch (start us, length us, event | category | flops | bytes accessed | tf_op | source)
XLA Modules:
  0.0 137.2 jit_solution(18180646118305252303)
XLA Ops:
  1.9 132.0 %heads.1 = bf16[16,2,16,1152]{3,2,1,0:T(8,128)(2,1)} custom-call(bf16[128,1792]{1,0:T(8,128)(2,1)} %fi_hbm.1, bf16[128,2048]{1,0:T(8,128)(2,1)} %ft_hbm.1, bf16[224,1152]{1,0:T(8,128)(2,1)} %wi_hbm.1, bf16[256,1152]{1,0:T(8,128)(2,1)} %wt_hbm.1, f32[1]{0:T(128)S(6)} %copy.8.ls, f32[1]{0:T(128)S(6)} %copy.9.lb), custom_call_target="tpu_custom_call" | custom-call | tf_op jit(solution)/shard_map/heads/pallas_call | solution.py:276
  134.0 0.0 slice-start
  134.0 0.0 slice-start.1
  134.0 1.0 slice-done
  135.0 1.1 bitcast_convert_fusion.1
  136.1 0.0 slice-done.1
  136.1 1.1 bitcast_convert_fusion
Async XLA Ops:
  134.0 1.0 slice-start
  134.0 2.1 %slice-start.1 = ((bf16[16,2,16,1152]{3,2,1,0:T(8,128)(2,1)}), bf16[8,2,16,1152]{3,2,1,0:T(8,128)(2,1)S(1)}, s32[]{:S(2)}) async-start(bf16[16,2,16,1152]{3,2,1,0:T(8,128)(2,1)} %heads.1), calls=%async_computation.1 | async-start | bytes 1179648 | tf_op jit(solution)/shard_map/slice | solution.py:305
